TPU v7x, 128 devices: a whole 4x4x4 slice. The times are simulated.
128 devices in a mesh: rows: 4 (over y_hi, core), loop: 32 (over z, x, y_lo).
Axes of the slice: x: 4, y: 4 (y_hi: 2, y_lo: 2; y = y_hi * 2 + y_lo), z: 4, core: 2. Of those that a mesh axis runs over, the one named last changes fastest.
Arguments:
- delta_weight_matrix: float32 [98304, 4096], P('rows', 'loop'), may hold values from -18 to 18
- offsets: int32 [2, 4], replicated, may hold values from 0 to 63, as said below
Outputs:
- rotated: float32 [98304, 4096], P('rows', 'loop')
Inputs may be any that keep to these rules, and one draw needn't show every extreme that they name: The 4 offsets of each step are distinct.
All inputs are finite; a program needn't handle non-finite values.
Results may differ from a plain program's by a relative error of at most 0.0003.
Values sent between devices are 32-bit elements; how exact they have to be, the bound alone decides.
No kernel may reach another device: no remote copies, remote signals or barrier semaphores. Data moves between devices by JAX's collectives and lax.ppermute only.
A program may use at most 128 MiB of HBM per device.

v0:
```python
import jax
import jax.numpy as jnp
from jax import lax
from jax.sharding import PartitionSpec as P

INNER_ROUNDS = 4
PRECISION_HIGH = lax.Precision.HIGHEST


def passed_along(shard, axis, by):
    devices = lax.axis_size(axis)
    pairs = [(i, i + by) for i in range(devices) if 0 <= i + by < devices]
    return lax.ppermute(shard, axis, pairs)


def paired_gram_matrix(left, right):
    return lax.dot_general(
        left,
        right,
        (((0,), (0,)), ((), ())),
        precision=PRECISION_HIGH,
        preferred_element_type=jnp.float32,
    )


def jacobi_rotations(gram_matrix, circle_shifts):
    block_width = gram_matrix.shape[0]
    half = block_width // 2
    right_vectors = jnp.eye(block_width, dtype=gram_matrix.dtype)
    column = jnp.arange(half, dtype=jnp.int32)
    for which in range(INNER_ROUNDS):
        partner = half + (column + circle_shifts[which]) % half
        g_first = gram_matrix[column, column]
        g_second = gram_matrix[partner, partner]
        g_cross = gram_matrix[column, partner]
        spread = g_second - g_first
        sign_part = jnp.where(spread >= 0.0, 1.0, -1.0).astype(gram_matrix.dtype)
        tangent = (
            sign_part
            * 2.0
            * g_cross
            / (jnp.abs(spread) + jnp.sqrt(spread * spread + 4.0 * g_cross * g_cross))
        )
        cosine = 1.0 / jnp.sqrt(1.0 + tangent * tangent)
        sine = -tangent * cosine
        rotate_pair = jnp.zeros((block_width, block_width), gram_matrix.dtype)
        rotate_pair = rotate_pair.at[column, column].set(cosine).at[partner, partner].set(cosine)
        rotate_pair = rotate_pair.at[partner, column].set(sine).at[column, partner].set(-sine)
        gram_matrix = jnp.dot(
            rotate_pair.T,
            jnp.dot(gram_matrix, rotate_pair, precision=PRECISION_HIGH),
            precision=PRECISION_HIGH,
        )
        right_vectors = jnp.dot(right_vectors, rotate_pair, precision=PRECISION_HIGH)
    return (right_vectors, gram_matrix)


def reduced_gram_matrix(column_block):
    return lax.psum(paired_gram_matrix(column_block, column_block), "rows")


def body(delta_weight_matrix, offsets):
    half = delta_weight_matrix.shape[1] // 2
    place = lax.axis_index("loop")
    count = lax.axis_size("loop")
    first_place = place == 0
    last_place = place == count - 1
    right_vectors, rotated_blocks = jacobi_rotations(
        reduced_gram_matrix(delta_weight_matrix), offsets[0]
    )
    advanced_blocks = jnp.dot(
        delta_weight_matrix,
        right_vectors,
        precision=PRECISION_HIGH,
        preferred_element_type=jnp.float32,
    )
    first_half = advanced_blocks[:, :half]
    second_half = advanced_blocks[:, half:]
    arrived_up = passed_along(jnp.where(first_place, second_half, first_half), "loop", 1)
    arrived_down = passed_along(second_half, "loop", -1)
    new_first = jnp.where(first_place, first_half, arrived_up)
    new_second = jnp.where(last_place, first_half, arrived_down)
    shifted_blocks = jnp.concatenate([new_first, new_second], 1)
    updated_gram_matrix = reduced_gram_matrix(shifted_blocks)
    updated_right_vectors, discarded_value = jacobi_rotations(updated_gram_matrix, offsets[1])
    return jnp.dot(
        shifted_blocks,
        updated_right_vectors,
        precision=PRECISION_HIGH,
        preferred_element_type=jnp.float32,
    )


def solution(mesh):
    placed = (P("rows", "loop"), P())
    return jax.shard_map(
        body, mesh=mesh, in_specs=placed, out_specs=P("rows", "loop"), check_vma=False
    )
```

profile of v0, /device:TPU:1, one launch (start us, length us, event | category | flops | bytes accessed | tf_op | source)
XLA Modules:
  0.0 632.7 jit_solution(15431990333249425547)
XLA Ops:
  6.5 28.9 %fusion.116 = f32[128,128]{1,0:T(8,128)} fusion(f32[24576,128]{1,0:T(8,128)} %param.2), kind=kOutput, calls=%fused_computation.285 | convolution fusion | flops 4831838208 | bytes 12648448 | tf_op jit(solution)/shard_map/dot_general | solution.py:17
  43.9 35.2 %all-reduce.3.cloned.1.call-done = f32[128,128]{1,0:T(8,128)} async-done(((f32[128,128]{1,0:T(8,128)}), f32[128,128]{1,0:T(8,128)}) %all-reduce.3.cloned.1.call-update) | async-done | bytes 65552 | tf_op jit(solution)/shard_map/psum | solution.py:59
  84.2 4.0 scatter_fusion
  88.2 3.8 scatter_fusion.1
  92.0 3.8 scatter_fusion.2
  95.8 3.8 scatter_fusion.3
  103.5 3.8 scatter_fusion.4
  114.9 3.8 scatter_fusion.7
  121.6 3.8 scatter_fusion.8
  125.4 3.8 scatter_fusion.9
  129.2 3.8 scatter_fusion.10
  133.0 4.2 scatter_fusion.11
  140.6 3.8 scatter_fusion.12
  144.4 3.8 scatter_fusion.13
  151.9 3.8 scatter_fusion.15
  156.0 17.3 %convolution_bitcast_fusion = f32[24576,128]{0,1:T(8,128)} fusion(f32[128,128]{1,0:T(8,128)S(1)} %fusion.125, f32[24576,128]{1,0:T(8,128)} %param.2), kind=kOutput, calls=%fused_computation.56 | convolution fusion | flops 4831838208 | bytes 25231360 | tf_op jit(solution)/shard_map/dot_general | solution.py:71
  173.2 10.4 %slice_select_fusion.2 = (f32[24576,64]{0,1:T(8,128)}, f32[24576,64]{0,1:T(8,128)}) fusion(f32[24576,128]{0,1:T(8,128)} %convolution_bitcast_fusion, pred[]{:T(512)S(6)} %eq.21), kind=kLoop, calls=%fused_computation.62 | loop fusion | flops 1572864 | bytes 25165824 | tf_op jit(solution)/shard_map/jit(_where)/select_n | solution.py:79
  183.6 4.9 collective-permute-start
  196.5 259.1 %collective-permute-done = f32[24576,64]{0,1:T(8,128)} collective-permute-done((f32[24576,64]{0,1:T(8,128)}, f32[24576,64]{0,1:T(8,128)}, u32[]{:S(2)}, u32[]{:S(2)}) %collective-permute-start) | collective-permute-done | bytes 6291488 | tf_op jit(solution)/shard_map/ppermute | solution.py:13
  455.7 5.5 collective-permute-done.1
  461.2 10.4 %slice_select_fusion.1 = (f32[24576,64]{0,1:T(8,128)}, f32[24576,64]{0,1:T(8,128)}) fusion(f32[24576,64]{0,1:T(8,128)} %collective-permute-done, f32[24576,128]{0,1:T(8,128)} %convolution_bitcast_fusion, pred[]{:T(512)S(6)} %eq.21, f32[24576,64]{0,1:T(8,128)} %collective-permute-done.1, pred[]{:T(512)S(6)} %eq.23), kind=kLoop, calls=%fused_computation.61 | loop fusion | flops 3145728 | bytes 31457282 | tf_op jit(solution)/shard_map/jit(_where)/select_n | solution.py:81
  471.5 14.8 %fusion.1 = f32[128,128]{1,0:T(8,128)} fusion(f32[24576,64]{0,1:T(8,128)} %get-tuple-element.30, f32[24576,64]{0,1:T(8,128)} %get-tuple-element.29), kind=kOutput, calls=%fused_computation.59 | convolution fusion | flops 4834983936 | bytes 12648448 | tf_op jit(solution)/shard_map/dot_general | solution.py:17
  487.0 37.9 %all-reduce.5.cloned.1.call-done = f32[128,128]{1,0:T(8,128)} async-done(((f32[128,128]{1,0:T(8,128)}), f32[128,128]{1,0:T(8,128)}) %all-reduce.5.cloned.1.call-update) | async-done | bytes 65552 | tf_op jit(solution)/shard_map/psum | solution.py:59
  530.1 3.8 scatter_fusion.16
  541.4 3.8 scatter_fusion.19
  549.2 3.8 scatter_fusion.20
  560.5 4.0 scatter_fusion.23
  567.5 3.8 scatter_fusion.24
  578.8 3.8 scatter_fusion.27
  586.0 3.8 scatter_fusion.28
  597.3 3.8 scatter_fusion.31
  601.3 24.1 %fusion = f32[24576,128]{1,0:T(8,128)} fusion(f32[128,128]{1,0:T(8,128)S(1)} %fusion.134, f32[24576,64]{0,1:T(8,128)} %get-tuple-element.30, f32[24576,64]{0,1:T(8,128)} %get-tuple-element.29), kind=kOutput, calls=%fused_computation.58 | convolution fusion | flops 4834983936 | bytes 25231360 | tf_op jit(solution)/shard_map/dot_general | solution.py:86
  (113 shorter events, 89.5 us)
Async XLA Ops:
  6.5 29.0 %copy-start = (s32[2,4]{1,0:T(2,128)S(1)}, s32[2,4]{1,0:T(2,128)}, u32[]{:S(2)}) copy-start(s32[2,4]{1,0:T(2,128)} %param.3) | copy-start | bytes 100
  6.5 72.5 %all-reduce.3.cloned.1.call-start = ((), (), s32[]{:S(2)}) async-start(), calls=%async_computation | async-start | bytes 131072 | tf_op jit(solution)/shard_map/psum | solution.py:59
  35.4 489.5 %all-reduce.5.cloned.1.call-start = ((), (), s32[]{:S(2)}) async-start(), calls=%async_computation.1 | async-start | bytes 131072 | tf_op jit(solution)/shard_map/psum | solution.py:59
  183.6 272.1 %collective-permute-start = (f32[24576,64]{0,1:T(8,128)}, f32[24576,64]{0,1:T(8,128)}, u32[]{:S(2)}, u32[]{:S(2)}) collective-permute-start(f32[24576,64]{0,1:T(8,128)} %get-tuple-element.31), channel_id=1, source_target_pairs={{0,1},{1,2},{2,3},{3,4},{4,5},{5,6},{6,7},{7,8},{8,9},{9,10},{10,1... | collective-permute-start | bytes 18874376 | tf_op jit(solution)/shard_map/ppermute | solution.py:13
  188.5 272.7 %collective-permute-start.1 = (f32[24576,64]{0,1:T(8,128)}, f32[24576,64]{0,1:T(8,128)}, u32[]{:S(2)}, u32[]{:S(2)}) collective-permute-start(f32[24576,64]{0,1:T(8,128)} %get-tuple-element.32), channel_id=1, source_target_pairs={{1,0},{2,1},{3,2},{4,3},{5,4},{6,5},{7,6},{8,7},{9,8},{10,9},{11,1... | collective-permute-start | bytes 18874376 | tf_op jit(solution)/shard_map/ppermute | solution.py:13
Sparse Core Ops, SparseCore 0:
  35.6 43.4 all-reduce.2
  486.5 38.4 all-reduce.4
where the time goes:
time: 642 us; the launch traced here: 633 us
  waiting for transfers between devices  338 us (53%)
  local copies, waits for them, and re-layouts  147 us (23%)
  matrix products  91.2 us (14%)
  other arithmetic  35.9 us (6%)
  between operations  14.5 us (2%)
    ppermute x2, waiting for transfers between devices, passed_along(): return lax.ppermute(shard, axis, pairs)  265 us
    psum x2, waiting for transfers between devices, reduced_gram_matrix(): return lax.psum(paired_gram_matrix(column_block, column_block), 'rows')  73.1 us
    scatter x16, local copies, waits for them, and re-layouts, jacobi_rotations(): rotate_pair.at[partner, column].set(sine).at[column, partner].set(-sine)  61.2 us
    scatter x16, local copies, waits for them, and re-layouts, jacobi_rotations(): rotate_pair.at[column, column].set(cosine).at[partner, partner].set(cosine)  60.7 us
    dot_general x2, matrix products, paired_gram_matrix(): lax.dot_general(left, right, (((0,), (0,)), ((), ())), precision=PRECISIO...  43.7 us
    dot_general x1, matrix products, body(): jnp.dot(shifted_blocks, updated_right_vectors, precision=PRECISION_HIGH,...  24.1 us
    dot_general x1, matrix products, body(): jnp.dot(delta_weight_matrix, right_vectors, precision=PRECISION_HIGH, pre...  17.3 us
  transfers between devices with their start and end apart: 4, of which 4 were waited for; matrix products, arithmetic and copies ran while one was open for 2% of the time, Pallas kernels for 0%

commit v1 on v0

--- a/solution.py
+++ b/solution.py
@@ -56,7 +56,7 @@
 
 
 def reduced_gram_matrix(column_block):
-    return lax.psum(paired_gram_matrix(column_block, column_block), "rows")
+    return jnp.sum(lax.all_gather(paired_gram_matrix(column_block, column_block), "rows"), axis=0)
 
 
 def body(delta_weight_matrix, offsets):

time: 642 us -> 564 us (0.88)
  waiting for transfers between devices: 338 us -> 263 us
  blocking collectives: 0 us -> 16.4 us
  between operations: 14.5 us -> 1.08 us
    psum x2 -> x0, waiting for transfers between devices: 73.1 us -> none  [reduced_gram_matrix(): return lax.psum(paired_gram_matrix(column_block, column_block), 'rows')]
    all_gather x0 -> x2, blocking collectives: none -> 16.4 us  [reduced_gram_matrix(): lax.all_gather(paired_gram_matrix(column_block, column_block), 'rows')]
  transfers between devices with their start and end apart: 4 -> 2, of which waited for: 4 -> 2; matrix products, arithmetic and copies ran while one was open for 2% -> 1% of each run, Pallas kernels for 0% -> 0%
where the time goes in v1:
time: 564 us; the launch traced here: 555 us
  waiting for transfers between devices  263 us (47%)
  local copies, waits for them, and re-layouts  143 us (25%)
  matrix products  87.9 us (16%)
  other arithmetic  36.1 us (6%)
  blocking collectives  16.4 us (3%)
  starting transfers between devices  7.16 us (1%)
    ppermute x2, waiting for transfers between devices, passed_along(): return lax.ppermute(shard, axis, pairs)  263 us
    scatter x16, local copies, waits for them, and re-layouts, jacobi_rotations(): rotate_pair.at[partner, column].set(sine).at[column, partner].set(-sine)  61.2 us
    scatter x16, local copies, waits for them, and re-layouts, jacobi_rotations(): rotate_pair.at[column, column].set(cosine).at[partner, partner].set(cosine)  60.8 us
    dot_general x2, matrix products, paired_gram_matrix(): lax.dot_general(left, right, (((0,), (0,)), ((), ())), precision=PRECISIO...  42.3 us
    dot_general x1, matrix products, body(): jnp.dot(shifted_blocks, updated_right_vectors, precision=PRECISION_HIGH,...  23.8 us
    dot_general x1, matrix products, body(): jnp.dot(delta_weight_matrix, right_vectors, precision=PRECISION_HIGH, pre...  17.3 us
    all_gather x2, blocking collectives, reduced_gram_matrix(): lax.all_gather(paired_gram_matrix(column_block, column_block), 'rows')  16.4 us
  transfers between devices with their start and end apart: 2, of which 2 were waited for; matrix products, arithmetic and copies ran while one was open for 1% of the time, Pallas kernels for 0%

profile of v1, /device:TPU:1, one launch (start us, length us, event | category | flops | bytes accessed | tf_op | source)
XLA Modules:
  0.0 554.7 jit_solution(15955554952179478274)
XLA Ops:
  9.5 28.3 %fusion.116 = f32[128,128]{1,0:T(8,128)S(1)} fusion(f32[24576,128]{1,0:T(8,128)} %param.2), kind=kOutput, calls=%fused_computation.285 | convolution fusion | flops 4831838208 | bytes 12648448 | tf_op jit(solution)/shard_map/dot_general | solution.py:17
  37.8 8.8 %all-gather = f32[512,128]{1,0:T(8,128)S(1)} all-gather(f32[128,128]{1,0:T(8,128)S(1)} %fusion.116), channel_id=2, replica_groups=mesh['rows'=4,'loop'=32] {'rows'}, dimensions={0}, use_global_device_ids=true | all-gather | bytes 327680 | tf_op jit(solution)/shard_map/all_gather | solution.py:59
  49.0 4.0 scatter_fusion
  56.8 3.8 scatter_fusion.2
  60.6 3.8 scatter_fusion.3
  67.5 3.8 scatter_fusion.4
  78.9 3.8 scatter_fusion.7
  85.6 3.8 scatter_fusion.8
  89.4 3.8 scatter_fusion.9
  93.2 3.8 scatter_fusion.10
  97.0 4.3 scatter_fusion.11
  104.6 3.8 scatter_fusion.12
  108.4 3.8 scatter_fusion.13
  116.0 3.8 scatter_fusion.15
  120.0 17.3 %convolution_bitcast_fusion = f32[24576,128]{0,1:T(8,128)} fusion(f32[128,128]{1,0:T(8,128)S(1)} %fusion.125, f32[24576,128]{1,0:T(8,128)} %param.2), kind=kOutput, calls=%fused_computation.56 | convolution fusion | flops 4831838208 | bytes 25231360 | tf_op jit(solution)/shard_map/dot_general | solution.py:71
  137.3 10.4 %slice_select_fusion.2 = (f32[24576,64]{0,1:T(8,128)}, f32[24576,64]{0,1:T(8,128)}) fusion(f32[24576,128]{0,1:T(8,128)} %convolution_bitcast_fusion, pred[]{:T(512)S(6)} %eq.21), kind=kLoop, calls=%fused_computation.62 | loop fusion | flops 1572864 | bytes 25165824 | tf_op jit(solution)/shard_map/jit(_where)/select_n | solution.py:79
  147.6 5.7 %collective-permute-start = (f32[24576,64]{0,1:T(8,128)}, f32[24576,64]{0,1:T(8,128)}, u32[]{:S(2)}, u32[]{:S(2)}) collective-permute-start(f32[24576,64]{0,1:T(8,128)} %get-tuple-element.31), channel_id=1, source_target_pairs={{0,1},{1,2},{2,3},{3,4},{4,5},{5,6},{6,7},{7,8},{8,9},{9,10},{10,1... | collective-permute-start | bytes 18874376 | tf_op jit(solution)/shard_map/ppermute | solution.py:13
  162.2 258.3 %collective-permute-done = f32[24576,64]{0,1:T(8,128)} collective-permute-done((f32[24576,64]{0,1:T(8,128)}, f32[24576,64]{0,1:T(8,128)}, u32[]{:S(2)}, u32[]{:S(2)}) %collective-permute-start) | collective-permute-done | bytes 6291488 | tf_op jit(solution)/shard_map/ppermute | solution.py:13
  420.6 5.0 collective-permute-done.1
  425.6 10.4 %slice_select_fusion.1 = (f32[24576,64]{0,1:T(8,128)}, f32[24576,64]{0,1:T(8,128)}) fusion(f32[24576,64]{0,1:T(8,128)} %collective-permute-done, f32[24576,128]{0,1:T(8,128)} %convolution_bitcast_fusion, pred[]{:T(512)S(6)} %eq.21, f32[24576,64]{0,1:T(8,128)} %collective-permute-done.1, pred[]{:T(512)S(6)} %eq.23), kind=kLoop, calls=%fused_computation.61 | loop fusion | flops 3145728 | bytes 31457282 | tf_op jit(solution)/shard_map/jit(_where)/select_n | solution.py:81
  435.9 14.0 %fusion.1 = f32[128,128]{1,0:T(8,128)S(1)} fusion(f32[24576,64]{0,1:T(8,128)} %get-tuple-element.30, f32[24576,64]{0,1:T(8,128)} %get-tuple-element.29), kind=kOutput, calls=%fused_computation.59 | convolution fusion | flops 4834983936 | bytes 12648448 | tf_op jit(solution)/shard_map/dot_general | solution.py:17
  450.0 7.6 %all-gather.1 = f32[512,128]{1,0:T(8,128)S(1)} all-gather(f32[128,128]{1,0:T(8,128)S(1)} %fusion.1), channel_id=3, replica_groups=mesh['rows'=4,'loop'=32] {'rows'}, dimensions={0}, use_global_device_ids=true | all-gather | bytes 327680 | tf_op jit(solution)/shard_map/all_gather | solution.py:59
  460.0 3.8 scatter_fusion.16
  471.4 3.8 scatter_fusion.19
  478.3 3.8 scatter_fusion.20
  482.1 3.8 scatter_fusion.21
  489.7 3.8 scatter_fusion.23
  496.4 3.8 scatter_fusion.24
  507.7 4.0 scatter_fusion.27
  515.1 3.8 scatter_fusion.28
  526.5 3.8 scatter_fusion.31
  530.5 23.8 %fusion = f32[24576,128]{1,0:T(8,128)} fusion(f32[128,128]{1,0:T(8,128)S(1)} %fusion.134, f32[24576,64]{0,1:T(8,128)} %get-tuple-element.30, f32[24576,64]{0,1:T(8,128)} %get-tuple-element.29), kind=kOutput, calls=%fused_computation.58 | convolution fusion | flops 4834983936 | bytes 25231360 | tf_op jit(solution)/shard_map/dot_general | solution.py:86
  (109 shorter events, 83.6 us)
Async XLA Ops:
  147.6 272.9 %collective-permute-start = (f32[24576,64]{0,1:T(8,128)}, f32[24576,64]{0,1:T(8,128)}, u32[]{:S(2)}, u32[]{:S(2)}) collective-permute-start(f32[24576,64]{0,1:T(8,128)} %get-tuple-element.31), channel_id=1, source_target_pairs={{0,1},{1,2},{2,3},{3,4},{4,5},{5,6},{6,7},{7,8},{8,9},{9,10},{10,1... | collective-permute-start | bytes 18874376 | tf_op jit(solution)/shard_map/ppermute | solution.py:13
  153.3 272.2 %collective-permute-start.1 = (f32[24576,64]{0,1:T(8,128)}, f32[24576,64]{0,1:T(8,128)}, u32[]{:S(2)}, u32[]{:S(2)}) collective-permute-start(f32[24576,64]{0,1:T(8,128)} %get-tuple-element.32), channel_id=1, source_target_pairs={{1,0},{2,1},{3,2},{4,3},{5,4},{6,5},{7,6},{8,7},{9,8},{10,9},{11,1... | collective-permute-start | bytes 18874376 | tf_op jit(solution)/shard_map/ppermute | solution.py:13
